TPU v7x, 32 devices: a whole 2x2x4 slice. The times are simulated.
32 devices in a mesh: parts: 2 (over y), replica: 8 (over z, core), tensor: 2 (over x).
Axes of the slice: x: 2, y: 2, z: 4, core: 2. Of those that a mesh axis runs over, the one named last changes fastest.
Arguments:
- queries: bfloat16 [4, 2048, 4096], P(None, ('parts', 'replica'), 'tensor'), parts along dimension 1, may hold values from -9 to 9
- step_keys: bfloat16 [4, 2048, 1024], P(None, ('parts', 'replica'), 'tensor'), parts along dimension 1, may hold values from -4 to 4
- step_values: bfloat16 [4, 2048, 1024], P(None, ('parts', 'replica'), 'tensor'), parts along dimension 1, may hold values from -4 to 4
- cached_key_rows: bfloat16 [2048, 8, 32, 128], P(('parts', 'replica'), 'tensor'), parts along dimension 0, may hold values from -4 to 4
- cached_value_rows: bfloat16 [2048, 8, 32, 128], P(('parts', 'replica'), 'tensor'), parts along dimension 0, may hold values from -4 to 4
- cache_length: int32 [2048], P(('parts', 'replica')), parts along dimension 0, may hold values from 2 to 32
- output_weight: bfloat16 [4096, 8192], P(None, 'tensor'), may hold values from -0.09375 to 0.09375
- adapter_down_bank: bfloat16 [256, 16, 4096], P(('parts', 'replica'), None, 'tensor'), parts along dimension 0, may hold values from -0.09375 to 0.09375
- adapter_up_bank: bfloat16 [256, 16, 8192], P(('parts', 'replica'), None, 'tensor'), parts along dimension 0, may hold values from -1.5 to 1.5
- adapter_bank_row: int32 [256], P('parts'), parts along dimension 0, may hold values from 0 to 127, as said below
- segment_adapter: int32 [16, 64], P(('parts', 'replica')), parts along dimension 0, may hold values from 0 to 127, as said below
- request_segment_index: int32 [16, 128], P(('parts', 'replica')), parts along dimension 0, may hold values from 0 to 63, never falling along the last dimension, each value on 1 to 6 neighbouring positions
Outputs:
- projected: bfloat16 [4, 2048, 8192], P(None, ('parts', 'replica'), 'tensor'), parts along dimension 1
There are 2 independent parts, one for each index of `parts`. A program takes and returns all parts, laid end to end along the dimension named above; an argument that names none is the same for every part. Nothing has to cross between parts.
Inputs may be any that keep to these rules, and one draw needn't show every extreme that they name: `adapter_bank_row`: a permutation of the 128 bank rows. `segment_adapter`: each row lists 64 distinct adapters; in each row at most 16 of them have adapter_bank_row values in one aligned block of 16 bank rows, and some block of every row holds exactly 16. `request_segment_index`: each row's segment numbers never fall; every segment number of 0 to 63 holds 1 to 6 requests, one exactly 6.
All inputs are finite; a program needn't handle non-finite values.
Results may differ from a plain program's by a relative error of at most 0.0062.
Values may be sent and summed in bfloat16 or wider, within the bound.
A program may use at most 192 MiB of HBM per device.

v0:
```python
import math

import jax
import jax.numpy as jnp
from jax import lax
from jax.sharding import PartitionSpec as P

adapter_scale = 2.0


def attend(queries, step_keys, step_values, cached_key_rows, cached_value_rows, cache_length):
    step_count, batch_rows, width = queries.shape
    kv_count = cached_key_rows.shape[1]
    cache_rows = cached_key_rows.shape[2]
    head_dim = cached_key_rows.shape[3]
    grouped = width // (kv_count * head_dim)
    query_full = queries.reshape(step_count, batch_rows, kv_count, grouped, head_dim)
    scale_factor = 1.0 / math.sqrt(head_dim)
    cache_scores = (
        jnp.einsum(
            "sbgqd,bgpd->sbgqp", query_full, cached_key_rows, preferred_element_type=jnp.float32
        )
        * scale_factor
    )
    fresh_keys = step_keys.reshape(step_count, batch_rows, kv_count, head_dim)
    fresh_scores = (
        jnp.einsum("sbgqd,tbgd->sbgqt", query_full, fresh_keys, preferred_element_type=jnp.float32)
        * scale_factor
    )
    live_mask = jnp.arange(cache_rows)[None, :] < cache_length[:, None]
    cache_scores = jnp.where(live_mask[None, :, None, None, :], cache_scores, -1e30)
    causal = jnp.arange(step_count)[None, :] <= jnp.arange(step_count)[:, None]
    fresh_scores = jnp.where(causal[:, None, None, None, :], fresh_scores, -1e30)
    scores = jnp.concatenate([cache_scores, fresh_scores], axis=-1)
    top_score = jnp.max(scores, axis=-1, keepdims=True)
    raised = jnp.exp(scores - top_score)
    weights = (raised / jnp.sum(raised, axis=-1, keepdims=True)).astype(jnp.bfloat16)
    cache_part = jnp.einsum(
        "sbgqp,bgpd->sbgqd",
        weights[..., :cache_rows],
        cached_value_rows,
        preferred_element_type=jnp.float32,
    )
    fresh_values = step_values.reshape(step_count, batch_rows, kv_count, head_dim)
    fresh_part = jnp.einsum(
        "sbgqt,tbgd->sbgqd",
        weights[..., cache_rows:],
        fresh_values,
        preferred_element_type=jnp.float32,
    )
    return (cache_part + fresh_part).reshape(step_count, batch_rows, width).astype(jnp.bfloat16)


def lookup(table, positions):
    entries = table.shape[0]
    hits = positions[:, None] == jnp.arange(entries)[None, :]
    return jnp.sum(jnp.where(hits, table[None, :], 0), axis=1)


def apply_rows(attention_output, shrink_rows, expand_rows):
    partial_value = jnp.einsum(
        "iuf,uof->iuo", attention_output, shrink_rows, preferred_element_type=jnp.float32
    )
    shrunk_features = lax.psum(partial_value, "tensor").astype(jnp.bfloat16)
    return jnp.einsum(
        "fuz,uzy->fuy", shrunk_features, expand_rows, preferred_element_type=jnp.float32
    )


def shards(
    queries,
    step_keys,
    step_values,
    cached_key_rows,
    cached_value_rows,
    cache_length,
    output_weight,
    adapter_down_bank,
    adapter_up_bank,
    adapter_bank_row,
    segment_adapter,
    request_segment_index,
):
    step_count, batch_rows, width = queries.shape
    attention_output = attend(
        queries, step_keys, step_values, cached_key_rows, cached_value_rows, cache_length
    )
    segment_ids = request_segment_index[0]
    wanted = segment_adapter[0]
    bank_rows = lookup(adapter_bank_row, wanted)
    bank_down, bank_up = (
        lax.all_gather(adapter_down_bank, "replica", axis=0, tiled=True),
        lax.all_gather(adapter_up_bank, "replica", axis=0, tiled=True),
    )
    request_bank = lookup(bank_rows, segment_ids)
    shrink_rows = bank_down[request_bank]
    expand_rows = bank_up[request_bank]
    adapter_delta = apply_rows(attention_output, shrink_rows, expand_rows)
    flat_rows = attention_output.reshape(step_count * batch_rows, width)
    base_projection = jnp.dot(
        lax.all_gather(flat_rows, "tensor", axis=1, tiled=True),
        output_weight,
        preferred_element_type=jnp.float32,
    )
    base_projection = base_projection.reshape(step_count, batch_rows, output_weight.shape[1])
    return (base_projection + adapter_scale * adapter_delta).astype(jnp.bfloat16)


def solution(mesh):
    return jax.shard_map(
        shards,
        mesh=mesh,
        in_specs=(
            P(None, ("parts", "replica"), "tensor"),
            P(None, ("parts", "replica"), "tensor"),
            P(None, ("parts", "replica"), "tensor"),
            P(("parts", "replica"), "tensor", None, None),
            P(("parts", "replica"), "tensor", None, None),
            P(("parts", "replica")),
            P(None, "tensor"),
            P(("parts", "replica"), None, "tensor"),
            P(("parts", "replica"), None, "tensor"),
            P("parts"),
            P(("parts", "replica"), None),
            P(("parts", "replica"), None),
        ),
        out_specs=P(None, ("parts", "replica"), "tensor"),
        check_vma=False,
    )
```

profile of v0, /device:TPU:0, one launch (start us, length us, event | category | flops | bytes accessed | tf_op | source)
XLA Modules:
  0.0 404.9 jit_solution(12006103306756045019)
XLA Ops:
  6.5 4.5 %reshape.69 = bf16[4,128,4,4,128]{4,3,2,1,0:T(4,128)(2,1)} reshape(bf16[4,128,2048]{2,1,0:T(8,128)(2,1)} %param.12) | data formatting | bytes 4194304 | tf_op jit(solution)/shard_map/reshape | solution.py:17
  11.0 0.1 reshape.70
  11.2 0.1 iota_compare_fusion
  11.3 5.8 %fusion.27 = (f32[4,128,4,4]{3,0,2,1:T(4,128)}, f32[4,128,4,4,4]{4,3,0,2,1:T(4,128)S(1)}) fusion(bf16[4,128,4,4,128]{4,3,2,1,0:T(4,128)(2,1)} %reshape.69, bf16[4,128,4,128,1]{3,2,1,0,4:T(4,128)(2,1)S(1)} %bitcast.49, pred[4,4]{1,0:T(4,128)(4,1)S(1)} %iota_compare_fusion.3), kind=kOutput, calls=%fused_computation.37 | convolution fusion | flops 8478720 | bytes 2785296 | tf_op jit(solution)/shard_map/sbgqd,tbgd->sbgqt/dot_general | solution.py:27
  17.1 10.0 %fusion.26 = (f32[4,128,4,4]{3,0,2,1:T(4,128)}, f32[4,128,4,4,32]{4,3,0,2,1:T(4,128)}) fusion(bf16[4,128,4,4,128]{4,3,2,1,0:T(4,128)(2,1)} %reshape.69, bf16[128,4,32,128]{3,2,1,0:T(8,128)(2,1)} %param.15, pred[128,32]{1,0:T(8,128)(4,1)S(1)} %iota_compare_fusion), kind=kOutput, calls=%fused_computation.36 | convolution fusion | flops 67887104 | bytes 7376896 | tf_op jit(solution)/shard_map/sbgqd,bgpd->sbgqp/dot_general | solution.py:20
  27.1 1.8 reduce_max.22
  29.0 17.2 %fusion.25 = f32[4,128,4,4]{3,0,2,1:T(4,128)S(1)} fusion(f32[4,128,4,4]{3,0,2,1:T(4,128)S(1)} %reduce_max.22, f32[4,128,4,4,4]{4,3,0,2,1:T(4,128)S(1)} %get-tuple-element.8, f32[4,128,4,4,32]{4,3,0,2,1:T(4,128)} %get-tuple-element.6), kind=kLoop, calls=%fused_computation.35 | loop fusion | flops 876544 | bytes 1245184 | tf_op jit(solution)/shard_map/reduce_sum | solution.py:37
  46.3 8.5 %divide_convert_fusion = bf16[4,128,4,4,36]{4,3,0,2,1:T(4,128)(2,1)S(1)} fusion(f32[4,128,4,4]{3,0,2,1:T(4,128)S(1)} %fusion.25, f32[4,128,4,4]{3,0,2,1:T(4,128)S(1)} %reduce_max.22, f32[4,128,4,4,4]{4,3,0,2,1:T(4,128)} %copy-done.1, f32[4,128,4,4,32]{4,3,0,2,1:T(4,128)S(1)} %copy-done.2), kind=kLoop, calls=%fused_computation.14 | loop fusion | flops 1179648 | bytes 1835008 | tf_op jit(solution)/shard_map/convert_element_type | solution.py:37
  54.8 0.1 reshape.71
  54.9 1.2 copy-done
  56.1 2.1 fusion.10
  58.1 3.1 fusion.13
  61.3 2.0 copy.52
  63.3 4.5 %convert_element_type.26 = bf16[512,2048]{1,0:T(8,128)(2,1)} reshape(bf16[4,128,4,4,128]{4,3,2,1,0:T(4,128)(2,1)} %copy.52) | data formatting | bytes 4194304 | tf_op jit(solution)/shard_map/convert_element_type | solution.py:51
  67.8 0.0 all-gather.8.cloned.1.call-start
  67.8 0.7 all-gather.8.cloned.1.call-update
  68.6 0.0 all-gather.6.cloned.1.call-start
  68.6 0.7 all-gather.6.cloned.1.call-update
  69.3 3.4 copy.53
  72.7 3.4 copy.54
  76.1 0.2 select_reduce_fusion.1
  76.3 0.1 select_reduce_fusion
  76.4 51.0 %all-gather.4.cloned.1.call-done = bf16[512,4096]{1,0:T(8,128)(2,1)} async-done(((bf16[512,2048]{1,0:T(8,128)(2,1)}), bf16[512,4096]{1,0:T(8,128)(2,1)}) %all-gather.4.cloned.1.call-update) | async-done | bytes 4194320 | tf_op jit(solution)/shard_map/all_gather | solution.py:101
  127.4 24.2 %fusion.28 = f32[512,4096]{1,0:T(8,128)} fusion(bf16[512,4096]{1,0:T(8,128)(2,1)} %all-gather.4.cloned.1.call-done, bf16[4096,4096]{1,0:T(8,128)(2,1)} %param.18), kind=kOutput, calls=%fused_computation.38 | convolution fusion | flops 17179869184 | bytes 46137344 | tf_op jit(solution)/shard_map/dot_general | solution.py:100
  151.6 59.5 %all-gather.8.cloned.1.call-done = bf16[128,16,2048]{2,1,0:T(8,128)(2,1)} async-done(((bf16[16,16,2048]{2,1,0:T(8,128)(2,1)}), bf16[128,16,2048]{2,1,0:T(8,128)(2,1)}) %all-gather.8.cloned.1.call-update) | async-done | bytes 8388624 | tf_op jit(solution)/shard_map/all_gather | solution.py:92
  211.1 10.6 %gather_fusion.1 = bf16[128,16,2048]{2,1,0:T(8,128)(2,1)} fusion(bf16[128,16,2048]{2,1,0:T(8,128)(2,1)} %all-gather.8.cloned.1.call-done, s32[1024]{0:T(1024)S(1)} %pad_clamp_fusion), kind=kCustom, calls=%fused_computation.1 | custom fusion | bytes 16777728 | tf_op jit(solution)/shard_map/gather | solution.py:96
  221.7 7.6 %convolution_bitcast_fusion = f32[4,128,16]{2,0,1:T(4,128)S(1)} fusion(bf16[128,16,2048]{2,1,0:T(8,128)(2,1)} %gather_fusion.1, bf16[4,128,2048]{2,0,1:T(4,128)(2,1)S(1)} %copy.54), kind=kOutput, calls=%fused_computation.21 | convolution fusion | flops 33554432 | bytes 10518528 | tf_op jit(solution)/shard_map/iuf,uof->iuo/dot_general | solution.py:61
  229.3 12.3 %psum.7 = bf16[4,128,16]{2,0,1:T(4,128)(2,1)S(1)} all-reduce(f32[4,128,16]{2,0,1:T(4,128)S(1)} %convolution_bitcast_fusion), channel_id=1, replica_groups=mesh['parts'=2,'replica'=8,'tensor'=2] {'tensor'}, use_global_device_ids=true, to_apply=%region_5.6 | all-reduce | flops 8192 | bytes 49152 | tf_op jit(solution)/shard_map/psum | solution.py:64
  241.6 120.8 %all-gather.6.cloned.1.call-done = bf16[128,16,4096]{2,1,0:T(8,128)(2,1)} async-done(((bf16[16,16,4096]{2,1,0:T(8,128)(2,1)}), bf16[128,16,4096]{2,1,0:T(8,128)(2,1)}) %all-gather.6.cloned.1.call-update) | async-done | bytes 16777232 | tf_op jit(solution)/shard_map/all_gather | solution.py:93
  362.4 14.3 %gather_fusion = bf16[128,16,4096]{2,1,0:T(8,128)(2,1)} fusion(bf16[128,16,4096]{2,1,0:T(8,128)(2,1)} %all-gather.6.cloned.1.call-done, s32[1024]{0:T(1024)S(1)} %pad_clamp_fusion), kind=kCustom, calls=%fused_computation | custom fusion | bytes 33554944 | tf_op jit(solution)/shard_map/gather | solution.py:97
  376.7 9.1 %fusion.29 = f32[128,4096,4]{1,2,0:T(4,128)} fusion(bf16[128,16,4096]{2,1,0:T(8,128)(2,1)} %gather_fusion, bf16[4,128,16]{2,0,1:T(4,128)(2,1)S(1)} %psum.7), kind=kOutput, calls=%fused_computation.39 | convolution fusion | flops 67108864 | bytes 25182208 | tf_op jit(solution)/shard_map/fuz,uzy->fuy/dot_general | solution.py:65
  385.8 12.6 %fusion = bf16[4,128,4096]{2,1,0:T(8,128)(2,1)} fusion(f32[4,128,4096]{2,1,0:T(8,128)} %bitcast.46, f32[128,4096,4]{1,2,0:T(4,128)} %fusion.29), kind=kLoop, calls=%fused_computation.3 | loop fusion | flops 6291456 | bytes 20971520 | tf_op jit(solution)/shard_map/convert_element_type | solution.py:106
  (24 shorter events, 0.1 us)
Async XLA Ops:
  6.5 4.5 %copy-start.4 = (bf16[4,128,512]{2,1,0:T(8,128)(2,1)S(1)}, bf16[4,128,512]{2,1,0:T(8,128)(2,1)}, u32[]{:S(2)}) copy-start(bf16[4,128,512]{2,1,0:T(8,128)(2,1)} %param.13) | copy-start | bytes 1572868
  6.5 4.6 %copy-start.6 = (s32[128]{0:T(128)S(1)}, s32[128]{0:T(128)}, u32[]{:S(2)}) copy-start(s32[128]{0:T(128)} %param.17) | copy-start | bytes 1540
  6.5 120.9 %all-gather.4.cloned.1.call-start = ((), (), s32[]{:S(2)}) async-start(), calls=%async_computation | async-start | bytes 6291456 | tf_op jit(solution)/shard_map/all_gather | solution.py:101
  17.1 11.9 %copy-start.1 = (f32[4,128,4,4,4]{4,3,0,2,1:T(4,128)}, f32[4,128,4,4,4]{4,3,0,2,1:T(4,128)S(1)}, u32[]{:S(2)}) copy-start(f32[4,128,4,4,4]{4,3,0,2,1:T(4,128)S(1)} %get-tuple-element.8) | copy-start | bytes 393220
  29.0 17.3 %copy-start.2 = (f32[4,128,4,4,32]{4,3,0,2,1:T(4,128)S(1)}, f32[4,128,4,4,32]{4,3,0,2,1:T(4,128)}, u32[]{:S(2)}) copy-start(f32[4,128,4,4,32]{4,3,0,2,1:T(4,128)} %get-tuple-element.6) | copy-start | bytes 3145732
  46.2 8.5 %copy-start.5 = (bf16[4,128,512]{2,1,0:T(8,128)(2,1)S(1)}, bf16[4,128,512]{2,1,0:T(8,128)(2,1)}, u32[]{:S(2)}) copy-start(bf16[4,128,512]{2,1,0:T(8,128)(2,1)} %param.14) | copy-start | bytes 1572868
  54.7 1.3 copy-start
  54.9 3.3 copy-start.3
  67.8 143.3 %all-gather.8.cloned.1.call-start = ((), (), s32[]{:S(2)}) async-start(), calls=%async_computation.2 | async-start | bytes 9437184 | tf_op jit(solution)/shard_map/all_gather | solution.py:92
  68.6 293.8 %all-gather.6.cloned.1.call-start = ((), (), s32[]{:S(2)}) async-start(), calls=%async_computation.1 | async-start | bytes 18874368 | tf_op jit(solution)/shard_map/all_gather | solution.py:93
  69.3 6.8 %copy-start.7 = (s32[128]{0:T(128)S(1)}, s32[128]{0:T(128)}, u32[]{:S(2)}) copy-start(s32[128]{0:T(128)} %param.21) | copy-start | bytes 1540
  69.3 6.8 %copy-start.8 = (s32[1,64]{1,0:T(1,128)S(1)}, s32[1,64]{1,0:T(1,128)}, u32[]{:S(2)}) copy-start(s32[1,64]{1,0:T(1,128)} %param.22) | copy-start | bytes 772
  69.3 7.0 %copy-start.9 = (s32[1,128]{1,0:T(1,128)S(1)}, s32[1,128]{1,0:T(1,128)}, u32[]{:S(2)}) copy-start(s32[1,128]{1,0:T(1,128)} %param.23) | copy-start | bytes 1540
Sparse Core Ops, SparseCore 0:
  67.9 59.4 all-gather.3
  129.0 82.0 all-gather.7
  212.7 149.6 all-gather.5
where the time goes:
time: 406 us; the launch traced here: 405 us
  waiting for transfers between devices  233 us (57%)
  matrix products  62 us (15%)
  local copies, waits for them, and re-layouts  44.1 us (11%)
  other arithmetic  40.5 us (10%)
  between operations  13.3 us (3%)
  blocking collectives  12.3 us (3%)
    all_gather x1, waiting for transfers between devices, shards(): lax.all_gather(adapter_up_bank, 'replica', axis=0, tiled=True)  121 us
    all_gather x1, waiting for transfers between devices, shards(): lax.all_gather(adapter_down_bank, 'replica', axis=0, tiled=True)  59.5 us
    all_gather x1, waiting for transfers between devices, shards(): lax.all_gather(flat_rows, 'tensor', axis=1, tiled=True)  51 us
    dot_general x1, matrix products, shards(): jnp.dot(lax.all_gather(flat_rows, 'tensor', axis=1, tiled=True), output_w...  24.2 us
    reduce_sum x1, other arithmetic, attend(): jnp.sum(raised, axis=-1, keepdims=True)  17.2 us
    gather x1, local copies, waits for them, and re-layouts, shards(): expand_rows = bank_up[request_bank]  14.3 us
    convert_element_type x4, local copies, waits for them, and re-layouts, attend(): (cache_part + fresh_part).reshape(step_count, batch_rows, width)  13.3 us
    convert_element_type x1, other arithmetic, shards(): (base_projection + adapter_scale * adapter_delta).astype(jnp.bfloat16)  12.6 us
  transfers between devices with their start and end apart: 3, of which 3 were waited for; matrix products, arithmetic and copies ran while one was open for 12% of the time, Pallas kernels for 0%

commit v1 on v0

--- a/solution.py
+++ b/solution.py
@@ -57,14 +57,40 @@
     return jnp.sum(jnp.where(hits, table[None, :], 0), axis=1)
 
 
-def apply_rows(attention_output, shrink_rows, expand_rows):
-    partial_value = jnp.einsum(
-        "iuf,uof->iuo", attention_output, shrink_rows, preferred_element_type=jnp.float32
+def join_heads(rows):
+    if lax.axis_size("tensor") != 2:
+        return lax.all_gather(rows, "tensor", axis=1, tiled=True)
+    other = lax.ppermute(rows, "tensor", [(0, 1), (1, 0)])
+    first = lax.axis_index("tensor") == 0
+    halves = jnp.where(first, rows, other), jnp.where(first, other, rows)
+    return jnp.concatenate(halves, axis=1)
+
+
+def own_columns(request_bank, bank_size, rank):
+    owner_of_column = jnp.arange(bank_size * rank) // rank
+    return request_bank[:, None] == owner_of_column[None, :]
+
+
+def shrink(flat_rows, bank_down, request_bank, step_count):
+    bank_size, rank, width = bank_down.shape
+    products = jnp.dot(
+        flat_rows, bank_down.reshape(bank_size * rank, width).T, preferred_element_type=jnp.float32
     )
-    shrunk_features = lax.psum(partial_value, "tensor").astype(jnp.bfloat16)
-    return jnp.einsum(
-        "fuz,uzy->fuy", shrunk_features, expand_rows, preferred_element_type=jnp.float32
-    )
+    mine = own_columns(request_bank, bank_size, rank)
+    products = products.reshape(step_count, -1, bank_size * rank)
+    kept = jnp.where(mine[None], products, 0.0)
+    kept = kept.reshape(step_count, -1, bank_size * rank // 128, 128)
+    folded = jnp.sum(kept, axis=2)
+    partial_value = jnp.sum(folded.reshape(step_count, -1, 128 // rank, rank), axis=2)
+    return lax.psum(partial_value, "tensor").astype(jnp.bfloat16)
+
+
+def spread(shrunk, request_bank, bank_size):
+    rank = shrunk.shape[-1]
+    mine = own_columns(request_bank, bank_size, rank)
+    tiled = jnp.tile(shrunk, (1, 1, bank_size))
+    doubled = tiled * jnp.bfloat16(adapter_scale)
+    return jnp.where(mine[None], doubled, 0).reshape(-1, bank_size * rank)
 
 
 def shards(
@@ -88,22 +114,26 @@
     segment_ids = request_segment_index[0]
     wanted = segment_adapter[0]
     bank_rows = lookup(adapter_bank_row, wanted)
-    bank_down, bank_up = (
-        lax.all_gather(adapter_down_bank, "replica", axis=0, tiled=True),
-        lax.all_gather(adapter_up_bank, "replica", axis=0, tiled=True),
-    )
+    bank_down = lax.all_gather(adapter_down_bank, "replica", axis=0, tiled=True)
+    bank_up = lax.all_gather(adapter_up_bank, "replica", axis=0, tiled=True)
     request_bank = lookup(bank_rows, segment_ids)
-    shrink_rows = bank_down[request_bank]
-    expand_rows = bank_up[request_bank]
-    adapter_delta = apply_rows(attention_output, shrink_rows, expand_rows)
+    bank_size, rank, columns = bank_up.shape
     flat_rows = attention_output.reshape(step_count * batch_rows, width)
+    shrunk = shrink(flat_rows, bank_down, request_bank, step_count)
     base_projection = jnp.dot(
-        lax.all_gather(flat_rows, "tensor", axis=1, tiled=True),
+        join_heads(flat_rows),
         output_weight,
         preferred_element_type=jnp.float32,
     )
-    base_projection = base_projection.reshape(step_count, batch_rows, output_weight.shape[1])
-    return (base_projection + adapter_scale * adapter_delta).astype(jnp.bfloat16)
+    own_shrunk = spread(shrunk, request_bank, bank_size)
+    base_projection, own_shrunk = lax.optimization_barrier((base_projection, own_shrunk))
+    adapter_delta = jnp.dot(
+        own_shrunk,
+        bank_up.reshape(bank_size * rank, columns),
+        preferred_element_type=jnp.float32,
+    )
+    projected = (base_projection + adapter_delta).astype(jnp.bfloat16)
+    return projected.reshape(step_count, batch_rows, columns)
 
 
 def solution(mesh):

time: 406 us -> 269 us (0.66)
  waiting for transfers between devices: 233 us -> 126 us
  local copies, waits for them, and re-layouts: 44.1 us -> 21.8 us
  other arithmetic: 40.5 us -> 30.1 us
  matrix products: 62 us -> 66.2 us
    all_gather x3 -> x2, waiting for transfers between devices: 231 us -> 86.8 us  [the longest x1 86.8 us: shards(): bank_up = lax.all_gather(adapter_up_bank, 'replica', axis=0, tiled=True)]
    ppermute x0 -> x1, waiting for transfers between devices: none -> 37.5 us  [join_heads(): other = lax.ppermute(rows, 'tensor', [(0, 1), (1, 0)])]
    gather x2 -> x0, local copies, waits for them, and re-layouts: 24.9 us -> none  [the longest x1 14.3 us: shards(): expand_rows = bank_up[request_bank]]
    convert_element_type x1 -> x0, other arithmetic: 12.6 us -> none  [shards(): (base_projection + adapter_scale * adapter_delta).astype(jnp.bfloat16)]
    dot_general x3, matrix products: 40.9 us -> 47.1 us  [the longest x1 23.1 us: shards(): jnp.dot(join_heads(flat_rows), output_weight, preferred_element_type=jnp....]
    broadcast_in_dim x0 -> x2, local copies, waits for them, and re-layouts: none -> 4.69 us  [spread(): return jnp.where(mine[None], doubled, 0).reshape(-1, bank_size * rank)]
    convert_element_type x4 -> x3, local copies, waits for them, and re-layouts: 13.3 us -> 9.94 us  [attend(): (cache_part + fresh_part).reshape(step_count, batch_rows, width)]
  transfers between devices with their start and end apart: 3 -> 3, of which waited for: 3 -> 2; matrix products, arithmetic and copies ran while one was open for 12% -> 38% of each run, Pallas kernels for 0% -> 0%
where the time goes in v1:
time: 269 us
  waiting for transfers between devices  126 us (47%)
  matrix products  66.2 us (25%)
  other arithmetic  30.1 us (11%)
  local copies, waits for them, and re-layouts  21.8 us (8%)
  between operations  13.6 us (5%)
  blocking collectives  8.74 us (3%)
    all_gather x1, waiting for transfers between devices, shards(): bank_up = lax.all_gather(adapter_up_bank, 'replica', axis=0, tiled=True)  86.8 us
    ppermute x1, waiting for transfers between devices, join_heads(): other = lax.ppermute(rows, 'tensor', [(0, 1), (1, 0)])  37.5 us
    dot_general x1, matrix products, shards(): jnp.dot(join_heads(flat_rows), output_weight, preferred_element_type=jnp....  23.1 us
    reduce_sum x1, other arithmetic, attend(): jnp.sum(raised, axis=-1, keepdims=True)  17.3 us
    dot_general x1, matrix products, shards(): jnp.dot(own_shrunk, bank_up.reshape(bank_size * rank, columns), preferred...  17 us
    convert_element_type x3, local copies, waits for them, and re-layouts, attend(): (cache_part + fresh_part).reshape(step_count, batch_rows, width)  9.94 us
    dot_general x1, matrix products, attend(): jnp.einsum('sbgqd,bgpd->sbgqp', query_full, cached_key_rows, preferred_el...  9.53 us
    psum x1, blocking collectives, shrink(): return lax.psum(partial_value, 'tensor').astype(jnp.bfloat16)  8.74 us
  transfers between devices with their start and end apart: 3, of which 2 were waited for; matrix products, arithmetic and copies ran while one was open for 38% of the time, Pallas kernels for 0%

profile of v1, /device:TPU:0, one launch (start us, length us, event | category | flops | bytes accessed | tf_op | source)
XLA Modules:
  0.0 268.8 jit_solution(14813021836618942250)
XLA Ops:
  6.5 0.7 all-gather.3.cloned.1.call-update
  7.3 0.7 all-gather.5.cloned.1.call-update
  8.1 2.8 %reshape.119 = bf16[4,128,4,4,128]{4,3,2,1,0:T(4,128)(2,1)} reshape(bf16[4,128,2048]{2,1,0:T(8,128)(2,1)S(1)} %copy-done.3) | data formatting | bytes 4194304 | tf_op jit(solution)/shard_map/reshape | solution.py:17
  10.9 0.9 reshape.120
  11.8 1.2 reshape.121
  13.1 5.9 %fusion.31 = (f32[4,128,4,4]{3,0,2,1:T(4,128)}, f32[4,128,4,4,4]{4,3,0,2,1:T(4,128)S(1)}) fusion(bf16[4,128,4,4,128]{4,3,2,1,0:T(4,128)(2,1)} %reshape.119, bf16[4,128,4,128,1]{3,2,1,0,4:T(4,128)(2,1)} %bitcast.60, pred[4,4]{1,0:T(4,128)(4,1)S(1)} %iota_compare_fusion.3), kind=kOutput, calls=%fused_computation.46 | convolution fusion | flops 8478720 | bytes 2785296 | tf_op jit(solution)/shard_map/sbgqd,tbgd->sbgqt/dot_general | solution.py:27
  19.0 9.5 %fusion.30 = (f32[4,128,4,4]{3,0,2,1:T(4,128)}, f32[4,128,4,4,32]{4,3,0,2,1:T(4,128)}) fusion(bf16[4,128,4,4,128]{4,3,2,1,0:T(4,128)(2,1)} %reshape.119, bf16[128,4,32,128]{3,2,1,0:T(8,128)(2,1)} %param.15, pred[128,32]{1,0:T(8,128)(4,1)S(1)} %iota_compare_fusion), kind=kOutput, calls=%fused_computation.45 | convolution fusion | flops 67887104 | bytes 7376896 | tf_op jit(solution)/shard_map/sbgqd,bgpd->sbgqp/dot_general | solution.py:20
  28.6 1.8 reduce_max.22
  30.4 17.3 %fusion.29 = f32[4,128,4,4]{3,0,2,1:T(4,128)S(1)} fusion(f32[4,128,4,4]{3,0,2,1:T(4,128)S(1)} %reduce_max.22, f32[4,128,4,4,4]{4,3,0,2,1:T(4,128)S(1)} %get-tuple-element.14, f32[4,128,4,4,32]{4,3,0,2,1:T(4,128)} %get-tuple-element.12), kind=kLoop, calls=%fused_computation.44 | loop fusion | flops 876544 | bytes 1245184 | tf_op jit(solution)/shard_map/reduce_sum | solution.py:37
  47.7 7.4 %divide_convert_fusion = bf16[4,128,4,4,36]{4,3,0,2,1:T(4,128)(2,1)S(1)} fusion(f32[4,128,4,4]{3,0,2,1:T(4,128)S(1)} %fusion.29, f32[4,128,4,4]{3,0,2,1:T(4,128)S(1)} %reduce_max.22, f32[4,128,4,4,4]{4,3,0,2,1:T(4,128)S(1)} %get-tuple-element.14, f32[4,128,4,4,32]{4,3,0,2,1:T(4,128)S(1)} %copy-done), kind=kLoop, calls=%fused_computation.15 | loop fusion | flops 1179648 | bytes 1835008 | tf_op jit(solution)/shard_map/convert_element_type | solution.py:37
  55.1 2.2 fusion.13
  57.3 1.5 fusion.16
  58.8 2.0 copy.42
  60.8 4.6 %convert_element_type.29 = bf16[512,2048]{1,0:T(8,128)(2,1)} reshape(bf16[4,128,4,4,128]{4,3,2,1,0:T(4,128)(2,1)} %copy.42) | data formatting | bytes 4194304 | tf_op jit(solution)/shard_map/convert_element_type | solution.py:51
  65.4 2.6 collective-permute-start
  68.0 3.3 %copy.43 = bf16[4,128,4,4,128]{1,4,3,2,0:T(8,128)(2,1)} copy(bf16[4,128,4,4,128]{4,3,0,2,1:T(4,128)(2,1)S(1)} %fusion.16) | data formatting | bytes 4194304 | tf_op jit(solution)/shard_map/convert_element_type | solution.py:51
  71.4 0.2 select_reduce_fusion.1
  71.6 0.2 broadcast_compare_fusion
  71.9 1.6 broadcast_in_dim.98
  73.4 3.1 %copy.47 = pred[512,2048]{0,1:T(8,128)(4,1)S(1)} copy(pred[512,2048]{1,0:T(8,128)(4,1)} %bitcast.55) | data formatting | bytes 2097152 | tf_op jit(solution)/shard_map/jit(_where)/broadcast_in_dim | solution.py:93
  76.6 37.5 %collective-permute-done = bf16[512,2048]{1,0:T(8,128)(2,1)} collective-permute-done((bf16[512,2048]{1,0:T(8,128)(2,1)}, bf16[512,2048]{1,0:T(8,128)(2,1)}, u32[]{:S(2)}, u32[]{:S(2)}) %collective-permute-start) | collective-permute-done | bytes 2097184 | tf_op jit(solution)/shard_map/ppermute | solution.py:63
  114.1 1.9 broadcast_select_fusion.1
  116.0 23.1 %fusion.1 = f32[512,4096]{1,0:T(8,128)} fusion(bf16[4096,4096]{1,0:T(8,128)(2,1)} %param.18, bf16[512,2048]{1,0:T(8,128)(2,1)S(1)} %get-tuple-element.10, bf16[512,2048]{1,0:T(8,128)(2,1)S(1)} %get-tuple-element.9), kind=kOutput, calls=%fused_computation.4 | convolution fusion | flops 17188257792 | bytes 46137344 | tf_op jit(solution)/shard_map/dot_general | solution.py:123
  139.2 7.0 %convolution_select_fusion = f32[4,128,2048]{2,1,0:T(8,128)S(1)} fusion(bf16[4,128,2048]{1,2,0:T(8,128)(2,1)S(1)} %bitcast.57, bf16[2048,2048,1]{1,0,2:T(8,128)(2,1)} %bitcast.62, pred[128,2048]{1,0:T(8,128)(4,1)S(1)} %broadcast_compare_fusion), kind=kOutput, calls=%fused_computation.16 | convolution fusion | flops 4296015872 | bytes 14942208 | tf_op jit(solution)/shard_map/dot_general | solution.py:76
  146.2 0.9 copy.57
  147.1 0.7 bitcast_reduce_fusion
  147.8 0.1 copy.45
  147.9 8.7 %psum.7 = bf16[4,128,16]{1,2,0:T(8,128)(2,1)S(1)} all-reduce(f32[4,128,16]{1,2,0:T(8,128)S(1)} %reduce_sum.49), channel_id=1, replica_groups=mesh['parts'=2,'replica'=8,'tensor'=2] {'tensor'}, use_global_device_ids=true, to_apply=%region_7.8 | all-reduce | flops 8192 | bytes 49152 | tf_op jit(solution)/shard_map/psum | solution.py:85
  156.7 1.0 tile.2
  157.8 0.4 bitcast_select_fusion.1
  158.2 86.8 %all-gather.5.cloned.1.call-done = bf16[128,16,4096]{2,1,0:T(8,128)(2,1)} async-done(((bf16[16,16,4096]{2,1,0:T(8,128)(2,1)}), bf16[128,16,4096]{2,1,0:T(8,128)(2,1)}) %all-gather.5.cloned.1.call-update) | async-done | bytes 16777232 | tf_op jit(solution)/shard_map/all_gather | solution.py:118
  245.0 17.0 %add_convert_fusion = bf16[512,4096]{1,0:T(8,128)(2,1)} fusion(f32[512,4096]{1,0:T(8,128)} %fusion.1, bf16[512,2048]{0,1:T(8,128)(2,1)S(1)} %bitcast_select_fusion.1, bf16[2048,4096]{1,0:T(8,128)(2,1)} %bitcast.61), kind=kOutput, calls=%fused_computation | convolution fusion | flops 8594128896 | bytes 31457280 | tf_op jit(solution)/shard_map/dot_general | solution.py:130
  (30 shorter events, 0.5 us)
Async XLA Ops:
  6.5 1.6 copy-start.3
  6.5 4.3 %copy-start.5 = (bf16[4,128,512]{2,1,0:T(8,128)(2,1)S(1)}, bf16[4,128,512]{2,1,0:T(8,128)(2,1)}, u32[]{:S(2)}) copy-start(bf16[4,128,512]{2,1,0:T(8,128)(2,1)} %param.13) | copy-start | bytes 1572868
  6.5 132.6 %all-gather.3.cloned.1.call-start = ((), (), s32[]{:S(2)}) async-start(), calls=%async_computation | async-start | bytes 9437184 | tf_op jit(solution)/shard_map/all_gather | solution.py:117
  7.3 5.7 %copy-start.6 = (s32[128]{0:T(128)S(1)}, s32[128]{0:T(128)}, u32[]{:S(2)}) copy-start(s32[128]{0:T(128)} %param.17) | copy-start | bytes 1540
  7.3 237.8 %all-gather.5.cloned.1.call-start = ((), (), s32[]{:S(2)}) async-start(), calls=%async_computation.1 | async-start | bytes 18874368 | tf_op jit(solution)/shard_map/all_gather | solution.py:118
  30.4 17.3 %copy-start = (f32[4,128,4,4,32]{4,3,0,2,1:T(4,128)S(1)}, f32[4,128,4,4,32]{4,3,0,2,1:T(4,128)}, u32[]{:S(2)}) copy-start(f32[4,128,4,4,32]{4,3,0,2,1:T(4,128)} %get-tuple-element.12) | copy-start | bytes 3145732
  55.1 2.2 copy-start.2
  60.8 10.5 %copy-start.7 = (s32[128]{0:T(128)S(1)}, s32[128]{0:T(128)}, u32[]{:S(2)}) copy-start(s32[128]{0:T(128)} %param.21) | copy-start | bytes 1540
  60.8 10.5 %copy-start.8 = (s32[1,64]{1,0:T(1,128)S(1)}, s32[1,64]{1,0:T(1,128)}, u32[]{:S(2)}) copy-start(s32[1,64]{1,0:T(1,128)} %param.22) | copy-start | bytes 772
  60.8 10.7 %copy-start.9 = (s32[1,128]{1,0:T(1,128)S(1)}, s32[1,128]{1,0:T(1,128)}, u32[]{:S(2)}) copy-start(s32[1,128]{1,0:T(1,128)} %param.23) | copy-start | bytes 1540
  65.4 48.7 %collective-permute-start = (bf16[512,2048]{1,0:T(8,128)(2,1)}, bf16[512,2048]{1,0:T(8,128)(2,1)}, u32[]{:S(2)}, u32[]{:S(2)}) collective-permute-start(bf16[512,2048]{1,0:T(8,128)(2,1)} %convert_element_type.29), channel_id=1, source_target_pairs={{0,1},{1,0},{2,3},{3,2},{4,5},{5,4},{6,7},{7,6},{8,9},{9,8},{10,11... | collective-permute-start | bytes 6291464 | tf_op jit(solution)/shard_map/ppermute | solution.py:63
  71.3 42.8 %copy-start.1 = (bf16[512,2048]{1,0:T(8,128)(2,1)S(1)}, bf16[512,2048]{1,0:T(8,128)(2,1)}, u32[]{:S(2)}) copy-start(bf16[512,2048]{1,0:T(8,128)(2,1)} %convert_element_type.29) | copy-start | bytes 6291460
  116.0 23.2 %copy-start.4 = (bf16[4,128,4,4,128]{1,4,3,2,0:T(8,128)(2,1)S(1)}, bf16[4,128,4,4,128]{1,4,3,2,0:T(8,128)(2,1)}, u32[]{:S(2)}) copy-start(bf16[4,128,4,4,128]{1,4,3,2,0:T(8,128)(2,1)} %copy.43) | copy-start | bytes 6291460
Sparse Core Ops, SparseCore 0:
  9.0 84.7 all-gather.2
  95.3 149.6 all-gather.4
